TPU v7x, 32 devices: a whole 2x2x4 slice. The times are simulated.
32 devices in a mesh: rows: 8 (over z, x), tm: 4 (over y, core).
Axes of the slice: x: 2, y: 2, z: 4, core: 2. Of those that a mesh axis runs over, the one named last changes fastest.
Arguments:
- counts: int32 [8192, 2048], P('rows', 'tm'), may hold values from 0 to 3
- col_blocks: int32 [64, 24], P('rows'), may hold values from 0 to 63, as said below
- kernel: bfloat16 [64, 24, 128, 128], P('rows'), may hold values from -0.109375 to 0.109375
- mixing: float32 [8, 8192], P(None, 'rows'), may hold values from -6.3 to 6.3
- decay_rate: float32 [8], replicated, may hold values from 0.0001 to 0.04
- baseline: float32 [8192], P('rows'), may hold values from -6 to 6
Outputs:
- intensity: bfloat16 [8192, 2048], P('rows', 'tm')
Inputs may be any that keep to these rules, and one draw needn't show every extreme that they name: The 24 entries of a block row are different blocks, and each lies within two indices of rows of the row's own on either side, cyclically: (col_blocks[I, k] // 8 - I // 8) mod 8 is 0, 1, 2, 8 - 1 or 8 - 2.
All inputs are finite; a program needn't handle non-finite values.
Results may differ from a plain program's by a relative error of at most 0.0034.
Values may be sent and summed in bfloat16 or wider, within the bound.
A program may use at most 128 MiB of HBM per device.

v0:
```python
import jax
import jax.numpy as jnp
from jax import lax
from jax.sharding import PartitionSpec as P


def shifted(block, axis, distance):
    devices = range(lax.axis_size(axis))
    route = [((i - distance) % len(devices), i) for i in devices]
    return lax.ppermute(block, axis, route)


def carried_in(part, axis, combine, identity):
    place = lax.axis_index(axis)
    gathered = jax.tree.map(lambda a: lax.all_gather(a, axis), part)
    state = jax.tree.map(lambda a, e: jnp.zeros_like(a) + jnp.asarray(e, a.dtype), part, identity)

    def one(hop, state):
        return combine(
            state, jax.tree.map(lambda a: lax.dynamic_index_in_dim(a, hop, 0, False), gathered)
        )

    return lax.fori_loop(0, place, one, state)


def combine(earlier, subsequent):
    return (earlier[0] * subsequent[0], earlier[1] * subsequent[0] + subsequent[1])


def drive_window(values):
    pieces = []
    for offset in (2, 1, 0, -1, -2):
        if offset == 0:
            pieces.append(values)
        else:
            pieces.append(shifted(values, "rows", offset))
    return jnp.concatenate(pieces, axis=0)


def local(counts, col_blocks, kernel, mixing, decay_rate, baseline):
    n_types, panel_len = counts.shape
    block_len = min(128, panel_len)
    block_rows = col_blocks.shape[0]
    width = kernel.shape[2]
    bases = decay_rate.shape[0]
    highest = lax.Precision.HIGHEST
    amounts = counts.astype(jnp.float32)
    offsets = jnp.arange(block_len, dtype=jnp.float32)
    distance = offsets[None, :] - offsets[:, None]
    rate_col = decay_rate[:, None]
    toeplitz = jnp.where(
        distance[None] > 0,
        jnp.exp(-decay_rate[:, None, None] * jnp.maximum(distance, 0.0)[None]),
        0.0,
    )
    entry_decay = jnp.exp(-rate_col * offsets[None, :])
    exit_decay = jnp.exp(-rate_col * (block_len - offsets)[None, :])
    block_decay = jnp.exp(-rate_col * block_len)
    history = jnp.zeros((bases, n_types), jnp.float32)
    pieces = []
    for block in range(panel_len // block_len):
        segment = amounts[:, block * block_len : (block + 1) * block_len]
        inside = jnp.einsum("ns,bst->bnt", segment, toeplitz, precision=highest)
        pieces.append(inside + history[:, :, None] * entry_decay[:, None, :])
        history = block_decay * history + jnp.einsum(
            "ns,bs->bn", segment, exit_decay, precision=highest
        )
    state_inside = jnp.concatenate(pieces, axis=2)
    positions = jnp.arange(panel_len, dtype=jnp.float32)
    panel_entry = jnp.exp(-rate_col * positions[None, :])
    weighted = mixing * rate_col
    panel_step = jnp.exp(-rate_col * panel_len)
    scanned = carried_in(
        (panel_step, history), "tm", combine, (jnp.ones_like(panel_step), jnp.zeros_like(history))
    )
    incoming = scanned[1]
    states = state_inside + incoming[:, :, None] * panel_entry[:, None, :]
    driving = jnp.sum(weighted[:, :, None] * states, axis=0).astype(jnp.bfloat16)
    window = drive_window(driving)
    row_dev = lax.axis_index("rows")
    total_blocks = block_rows * lax.axis_size("rows")
    local_ids = jnp.mod(col_blocks - (row_dev - 2) * block_rows, total_blocks)
    window_blocks = window.reshape(5 * block_rows, width, panel_len)
    gathered = jnp.take(window_blocks, local_ids.reshape(-1), axis=0).reshape(
        block_rows, col_blocks.shape[1], width, panel_len
    )
    potential = jnp.einsum("ikab,ikbt->iat", kernel, gathered, preferred_element_type=jnp.float32)
    potential = potential.reshape(n_types, panel_len) + baseline[:, None]
    return jax.nn.softplus(potential).astype(jnp.bfloat16)


def solution(mesh):
    in_specs = (
        P("rows", "tm"),
        P("rows", None),
        P("rows", None, None, None),
        P(None, "rows"),
        P(),
        P("rows"),
    )
    out_specs = P("rows", "tm")
    return jax.shard_map(local, mesh=mesh, in_specs=in_specs, out_specs=out_specs, check_vma=False)
```

profile of v0, /device:TPU:16, one launch (start us, length us, event | category | flops | bytes accessed | tf_op | source)
XLA Modules:
  0.0 158.9 jit_solution(15202496123436869491)
XLA Ops:
  0.1 1.2 dynamic-slice
  2.0 0.8 exponential_dynamic-update-slice_fusion
  2.7 0.1 broadcast_multiply_fusion.1
  2.8 0.1 multiply_exponential_fusion
  2.9 1.8 %convert_element_type.9 = f32[1024,512]{1,0:T(8,128)S(1)} convert(s32[1024,512]{1,0:T(8,128)} %param.8) | non-fusion elementwise | flops 524288 | bytes 4194304 | tf_op jit(solution)/shard_map/convert_element_type | solution.py:47
  4.7 0.6 convolution_add_fusion.3
  5.3 0.6 convolution_add_fusion.2
  5.9 0.6 convolution_add_fusion.1
  6.4 0.6 convolution_add_fusion
  7.0 5.2 %bitcast_add_fusion.1 = f32[8,1024,128]{1,2,0:T(8,128)} fusion(f32[8,1024]{1,0:T(8,128)S(1)} %convolution_add_fusion.1, f32[8,128]{1,0:T(8,128)S(1)} %get-tuple-element.82, f32[1024,512]{1,0:T(8,128)S(1)} %convert_element_type.9, f32[128,128]{0,1:T(8,128)S(1)} %fusion.35, f32[8]{0:T(128)S(1)} %get-tuple-element.80, pred[128,128]{0,1:T(8,128)(4,1)S(1)} %fusion.36), kind=kOutput, calls=%fused_computation.11 | convolution fusion | flops 1612972032 | bytes 4837888 | tf_op jit(solution)/shard_map/ns,bst->bnt/dot_general | solution.py:63
  12.2 0.0 copy-start.1
  12.2 0.0 copy-start.4
  12.2 5.2 %bitcast_add_fusion.2 = f32[8,1024,128]{1,2,0:T(8,128)} fusion(f32[8,1024]{1,0:T(8,128)S(1)} %convolution_add_fusion.2, f32[8,128]{1,0:T(8,128)S(1)} %get-tuple-element.82, f32[1024,512]{1,0:T(8,128)S(1)} %convert_element_type.9, f32[128,128]{0,1:T(8,128)S(1)} %fusion.35, f32[8]{0:T(128)S(1)} %get-tuple-element.80, pred[128,128]{0,1:T(8,128)(4,1)S(1)} %fusion.36), kind=kOutput, calls=%fused_computation.12 | convolution fusion | flops 1612972032 | bytes 4837888 | tf_op jit(solution)/shard_map/ns,bst->bnt/dot_general | solution.py:63
  17.4 5.2 %bitcast_add_fusion.3 = f32[8,1024,128]{1,2,0:T(8,128)} fusion(f32[8,128]{1,0:T(8,128)S(1)} %get-tuple-element.82, f32[8,1024]{1,0:T(8,128)S(1)} %convolution_add_fusion.3, f32[1024,512]{1,0:T(8,128)S(1)} %convert_element_type.9, f32[128,128]{0,1:T(8,128)S(1)} %fusion.35, f32[8]{0:T(128)S(1)} %get-tuple-element.80, pred[128,128]{0,1:T(8,128)(4,1)S(1)} %fusion.36), kind=kOutput, calls=%fused_computation.13 | convolution fusion | flops 1612972032 | bytes 4837888 | tf_op jit(solution)/shard_map/ns,bst->bnt/dot_general | solution.py:63
  22.5 6.9 %all-reduce = f32[32]{0:T(128)S(1)} all-reduce(f32[32]{0:T(128)S(1)} %get-tuple-element.77), channel_id=2, replica_groups=mesh['rows'=8,'tm'=4] {'tm'}, use_global_device_ids=true, to_apply=%add | all-reduce | flops 32 | bytes 256
  29.4 0.1 reshape.136
  29.5 0.0 copy-done.1
  29.5 0.0 copy-done.4
  29.5 0.1 broadcast_multiply_fusion
  29.6 5.4 %all-gather.1 = f32[32,1024]{1,0:T(8,128)S(1)} all-gather(f32[8,1024]{1,0:T(8,128)S(1)} %convolution_add_fusion), channel_id=3, replica_groups=mesh['rows'=8,'tm'=4] {'tm'}, dimensions={0}, use_global_device_ids=true | all-gather | bytes 163840 | tf_op jit(solution)/shard_map/all_gather | solution.py:15
  35.0 0.0 copy-start
  35.0 3.5 %add_bitcast_fusion = f32[8,1024,128]{1,2,0:T(8,128)S(1)} fusion(f32[8,128]{1,0:T(8,128)S(1)} %get-tuple-element.81, f32[1024,512]{1,0:T(8,128)S(1)} %convert_element_type.9, f32[128,128]{0,1:T(8,128)S(1)} %fusion.35, f32[8]{0:T(128)S(1)} %get-tuple-element.80, pred[128,128]{0,1:T(8,128)(4,1)S(1)} %fusion.36), kind=kOutput, calls=%fused_computation.14 | convolution fusion | flops 1611923456 | bytes 4805120 | tf_op jit(solution)/shard_map/ns,bst->bnt/dot_general | solution.py:63
  38.5 0.0 copy-done
  38.5 0.0 copy-start.3
  38.5 5.5 %fusion.4 = bf16[1024,512]{0,1:T(8,128)(2,1)S(1)} fusion(f32[8,1024,128]{1,2,0:T(8,128)S(1)} %copy-done, f32[8,1024,128]{1,2,0:T(8,128)} %bitcast_add_fusion.2, f32[8,1024,128]{1,2,0:T(8,128)} %bitcast_add_fusion.3, f32[8,1024,128]{1,2,0:T(8,128)S(1)} %add_bitcast_fusion, f32[8,512]{1,0:T(8,128)S(1)} %multiply_exponential_fusion, ...), kind=kLoop, calls=%fused_computation.8 | loop fusion | flops 28835840 | bytes 17907712 | tf_op jit(solution)/shard_map/reduce_sum | solution.py:78
  44.0 1.6 %collective-permute-start = (bf16[1024,512]{0,1:T(8,128)(2,1)S(1)}, bf16[1024,512]{0,1:T(8,128)(2,1)}, u32[]{:S(2)}, u32[]{:S(2)}) collective-permute-start(bf16[1024,512]{0,1:T(8,128)(2,1)S(1)} %fusion.4), channel_id=1, source_target_pairs={{24,0},{28,4},{0,8},{4,12},{8,16},{12,20},{16,24},{20,28},{25,1},{... | collective-permute-start | bytes 3145736 | tf_op jit(solution)/shard_map/ppermute | solution.py:10
  45.6 1.5 collective-permute-start.1
  47.1 1.4 collective-permute-start.2
  48.6 0.5 collective-permute-start.3
  49.0 0.0 copy-done.3
  49.0 0.1 reshape.126
  49.1 65.5 %collective-permute-done = bf16[1024,512]{0,1:T(8,128)(2,1)} collective-permute-done((bf16[1024,512]{0,1:T(8,128)(2,1)S(1)}, bf16[1024,512]{0,1:T(8,128)(2,1)}, u32[]{:S(2)}, u32[]{:S(2)}) %collective-permute-start) | collective-permute-done | bytes 1048608 | tf_op jit(solution)/shard_map/ppermute | solution.py:10
  114.6 2.3 %constant_dynamic-update-slice_fusion.4 = bf16[5120,512]{0,1:T(8,128)(2,1)} fusion(bf16[1024,512]{0,1:T(8,128)(2,1)} %collective-permute-done), kind=kLoop, calls=%fused_computation.60 | loop fusion | bytes 2097152
  117.0 0.0 collective-permute-done.1
  117.0 2.3 %constant_dynamic-update-slice_fusion.3 = bf16[5120,512]{0,1:T(8,128)(2,1)} fusion(bf16[5120,512]{0,1:T(8,128)(2,1)} %constant_dynamic-update-slice_fusion.4, bf16[1024,512]{0,1:T(8,128)(2,1)} %collective-permute-done.1), kind=kLoop, calls=%fused_computation.59 | loop fusion | bytes 2097152
  119.3 1.1 constant_dynamic-update-slice_fusion.2
  120.4 0.0 collective-permute-done.2
  120.4 1.1 constant_dynamic-update-slice_fusion.1
  121.5 0.0 collective-permute-done.3
  121.5 1.1 constant_dynamic-update-slice_fusion
  122.6 7.9 %copy.11 = bf16[5120,512]{1,0:T(8,128)(2,1)} copy(bf16[5120,512]{0,1:T(8,128)(2,1)} %constant_dynamic-update-slice_fusion) | data formatting | bytes 10485760 | tf_op jit(solution)/shard_map/concatenate | solution.py:37
  130.6 13.6 %gather_fusion = bf16[192,128,512]{2,1,0:T(8,128)(2,1)} fusion(bf16[40,128,512]{2,1,0:T(8,128)(2,1)} %bitcast.44, s32[1024]{0:T(1024)S(1)} %pad_clamp_fusion), kind=kCustom, calls=%fused_computation | custom fusion | bytes 50332416 | tf_op jit(solution)/shard_map/jit(_take)/gather | solution.py:84
  144.1 0.0 copy-start.2
  144.2 12.6 %fusion = f32[8,512,128,1]{1,2,3,0:T(8,128)S(1)} fusion(bf16[8,24,128,128]{3,2,1,0:T(8,128)(2,1)} %param.10, bf16[8,24,128,512]{3,2,1,0:T(8,128)(2,1)} %bitcast.45, pred[8,24]{1,0:T(8,128)(4,1)S(1)} %get-tuple-element.75), kind=kOutput, calls=%fused_computation.3 | convolution fusion | flops 3233808384 | bytes 33554624 | tf_op jit(solution)/shard_map/ikab,ikbt->iat/dot_general | solution.py:87
  156.7 0.0 copy-done.2
  156.7 2.2 %fusion.6 = bf16[1024,512]{1,0:T(8,128)(2,1)} fusion(f32[8,512,128,1]{1,2,3,0:T(8,128)S(1)} %fusion, f32[1024]{0:T(1024)S(1)} %copy-done.2), kind=kLoop, calls=%fused_computation.15 | loop fusion | flops 4194304 | bytes 3149824 | tf_op jit(solution)/shard_map/convert_element_type | solution.py:89
  (9 shorter events, 0.1 us)
Async XLA Ops:
  12.2 17.3 %copy-start.1 = (f32[8,1024]{1,0:T(8,128)S(1)}, f32[8,1024]{1,0:T(8,128)}, u32[]{:S(2)}) copy-start(f32[8,1024]{1,0:T(8,128)} %param.11) | copy-start | bytes 98308
  12.2 17.3 %copy-start.4 = (f32[8]{0:T(128)S(1)}, f32[8]{0:T(128)}, u32[]{:S(2)}) copy-start(f32[8]{0:T(128)} %param.12) | copy-start | bytes 100
  35.0 3.5 %copy-start = (f32[8,1024,128]{1,2,0:T(8,128)S(1)}, f32[8,1024,128]{1,2,0:T(8,128)}, u32[]{:S(2)}) copy-start(f32[8,1024,128]{1,2,0:T(8,128)} %bitcast_add_fusion.1) | copy-start | bytes 12582916
  38.5 10.5 %copy-start.3 = (s32[8,24]{1,0:T(8,128)S(1)}, s32[8,24]{1,0:T(8,128)}, u32[]{:S(2)}) copy-start(s32[8,24]{1,0:T(8,128)} %param.9) | copy-start | bytes 2308
  44.0 70.6 %collective-permute-start = (bf16[1024,512]{0,1:T(8,128)(2,1)S(1)}, bf16[1024,512]{0,1:T(8,128)(2,1)}, u32[]{:S(2)}, u32[]{:S(2)}) collective-permute-start(bf16[1024,512]{0,1:T(8,128)(2,1)S(1)} %fusion.4), channel_id=1, source_target_pairs={{24,0},{28,4},{0,8},{4,12},{8,16},{12,20},{16,24},{20,28},{25,1},{... | collective-permute-start | bytes 3145736 | tf_op jit(solution)/shard_map/ppermute | solution.py:10
  45.6 71.3 %collective-permute-start.1 = (bf16[1024,512]{0,1:T(8,128)(2,1)S(1)}, bf16[1024,512]{0,1:T(8,128)(2,1)}, u32[]{:S(2)}, u32[]{:S(2)}) collective-permute-start(bf16[1024,512]{0,1:T(8,128)(2,1)S(1)} %fusion.4), channel_id=1, source_target_pairs={{28,0},{0,4},{4,8},{8,12},{12,16},{16,20},{20,24},{24,28},{29,1},{... | collective-permute-start | bytes 3145736 | tf_op jit(solution)/shard_map/ppermute | solution.py:10
  47.1 73.3 %collective-permute-start.2 = (bf16[1024,512]{0,1:T(8,128)(2,1)S(1)}, bf16[1024,512]{0,1:T(8,128)(2,1)S(1)}, u32[]{:S(2)}, u32[]{:S(2)}) collective-permute-start(bf16[1024,512]{0,1:T(8,128)(2,1)S(1)} %fusion.4), channel_id=1, source_target_pairs={{4,0},{8,4},{12,8},{16,12},{20,16},{24,20},{28,24},{0,28},{5,1},{9... | collective-permute-start | bytes 3145736 | tf_op jit(solution)/shard_map/ppermute | solution.py:10
  48.6 73.0 %collective-permute-start.3 = (bf16[1024,512]{0,1:T(8,128)(2,1)S(1)}, bf16[1024,512]{0,1:T(8,128)(2,1)S(1)}, u32[]{:S(2)}, u32[]{:S(2)}) collective-permute-start(bf16[1024,512]{0,1:T(8,128)(2,1)S(1)} %fusion.4), channel_id=1, source_target_pairs={{8,0},{12,4},{16,8},{20,12},{24,16},{28,20},{0,24},{4,28},{9,1},{1... | collective-permute-start | bytes 3145736 | tf_op jit(solution)/shard_map/ppermute | solution.py:10
  144.1 12.6 %copy-start.2 = (f32[1024]{0:T(1024)S(1)}, f32[1024]{0:T(1024)}, u32[]{:S(2)}) copy-start(f32[1024]{0:T(1024)} %param.13) | copy-start | bytes 12292
where the time goes:
time: 159 us
  waiting for transfers between devices  65.5 us (41%)
  matrix products  33.8 us (21%)
  local copies, waits for them, and re-layouts  31 us (19%)
  blocking collectives  12.3 us (8%)
  other arithmetic  10.6 us (7%)
  starting transfers between devices  5 us (3%)
    ppermute x4, waiting for transfers between devices, shifted(): return lax.ppermute(block, axis, route)  65.5 us
    dot_general x4, matrix products, local(): inside = jnp.einsum('ns,bst->bnt', segment, toeplitz, precision=highest)  19 us
    gather x1, local copies, waits for them, and re-layouts, local(): jnp.take(window_blocks, local_ids.reshape(-1), axis=0)  13.6 us
    dot_general x1, matrix products, local(): jnp.einsum('ikab,ikbt->iat', kernel, gathered, preferred_element_type=jnp...  12.6 us
    concatenate x2, local copies, waits for them, and re-layouts, drive_window(): return jnp.concatenate(pieces, axis=0)  9.05 us
    unnamed x16, local copies, waits for them, and re-layouts  8.18 us
    unnamed x1, blocking collectives  6.9 us
    reduce_sum x1, other arithmetic, local(): jnp.sum(weighted[:, :, None] * states, axis=0).astype(jnp.bfloat16)  5.46 us
  transfers between devices with their start and end apart: 4, of which 1 were waited for; matrix products, arithmetic and copies ran while one was open for 4% of the time, Pallas kernels for 0%

commit v1 on v0

v1 whole, which is shorter than its diff:
```python
import functools

import jax
import jax.numpy as jnp
from jax import lax
from jax.experimental import pallas as pl
from jax.experimental.pallas import tpu as pltpu
from jax.sharding import PartitionSpec as P

MESH = pl.DeviceIdType.MESH
F32 = jnp.float32
BF16 = jnp.bfloat16
LEN = 128
TILE = 256


def split(x):
    high = x.astype(BF16)
    return high, (x - high.astype(F32)).astype(BF16)


def body(
    n_rows, n_tm,
    decay_ref, cols_ref, counts_hbm, kernel_hbm, mixing_ref, baseline_ref, out_hbm,
    counts, amounts, blocks, dense, own, win, total, result, table, entry3, states, hist, leaving, columns,
    load_sem, out_sem, send_sem, recv_sem, pass_sem, hist_send, hist_recv,
):
    n_types, panel = counts.shape
    chunks = panel // LEN
    bases = mixing_ref.shape[0]
    n_blocks = blocks.shape[0] - 1
    brows, slots = cols_ref.shape
    width = n_types // brows
    row, col = lax.axis_index("rows"), lax.axis_index("tm")
    odd = lax.rem(row, 2)
    up, down = lax.rem(row + 2, n_rows), lax.rem(row + n_rows - 2, n_rows)
    mate = row + 1 - 2 * odd
    peers = [lax.rem(col + k, n_tm) for k in range(1, n_tm)]

    load_counts = pltpu.make_async_copy(counts_hbm, counts, load_sem.at[0])
    load_blocks = pltpu.make_async_copy(kernel_hbm, blocks.at[pl.ds(0, n_blocks)], load_sem.at[1])
    load_counts.start()
    load_blocks.start()

    barrier = pltpu.get_barrier_semaphore()
    for r in (up, down, mate):
        pl.semaphore_signal(barrier, inc=1, device_id=(r, col), device_id_type=MESH)
    for c in peers:
        pl.semaphore_signal(barrier, inc=1, device_id=(row, c), device_id_type=MESH)

    rates = [decay_ref[b] for b in range(bases)]
    basis_id = lax.broadcasted_iota(jnp.int32, (bases, LEN), 0)
    rate_tile = jnp.zeros((bases, LEN), F32)
    for b in range(bases):
        rate_tile = jnp.where(basis_id == b, rates[b], rate_tile)
    rate = rate_tile[:, 0:1]

    since = lax.broadcasted_iota(jnp.int32, (bases, panel), 1)
    exits = []
    for m in range(1, chunks + 1):
        gap = (LEN * m - since).astype(F32)
        exits.append(jnp.where(since < LEN * m, jnp.exp(-rate * jnp.maximum(gap, 0.0)), 0.0))
    exits_high, exits_low = split(jnp.concatenate(exits, axis=0))
    exit_table = jnp.concatenate([exits_high, exits_low], axis=0)

    load_counts.wait()
    amounts[...] = counts[...].astype(F32).astype(BF16)
    both = lax.dot_general(
        exit_table, amounts[...], (((1,), (1,)), ((), ())), preferred_element_type=F32
    )
    states[...] = both[: chunks * bases] + both[chunks * bases :]
    leaving[...] = states[(chunks - 1) * bases :, :]
    pl.semaphore_wait(barrier, 3 + n_tm - 1)

    hist_copies = []
    for k, c in enumerate(peers):
        copy = pltpu.make_async_remote_copy(
            src_ref=leaving, dst_ref=hist.at[col], send_sem=hist_send.at[k], recv_sem=hist_recv.at[col],
            device_id=(row, c), device_id_type=MESH,
        )
        copy.start()
        hist_copies.append(copy)

    distance = (
        lax.broadcasted_iota(jnp.int32, (LEN, LEN), 1) - lax.broadcasted_iota(jnp.int32, (LEN, LEN), 0)
    )
    lag = jnp.maximum(distance, 0).astype(F32)
    for b in range(bases):
        high, low = split(jnp.where(distance > 0, jnp.exp(-rates[b] * lag), 0.0))
        table[0:LEN, b * LEN : (b + 1) * LEN] = high
        table[LEN : 2 * LEN, b * LEN : (b + 1) * LEN] = low
    offset = lax.broadcasted_iota(jnp.int32, (bases, LEN), 1).astype(F32)
    entry_high, entry_low = split(jnp.exp(-rate_tile * offset))
    entry3[...] = jnp.concatenate([entry_high, entry_high, entry_low, entry_low], axis=0)
    weights = mixing_ref[...] * rate
    stacked = jnp.concatenate([weights, jnp.broadcast_to(baseline_ref[...], (bases, n_types))], axis=0)
    columns[...] = jnp.transpose(stacked)

    incoming = jnp.zeros((bases, n_types), F32)
    for k, c in enumerate(peers):
        pltpu.make_async_remote_copy(
            src_ref=leaving, dst_ref=hist.at[c], send_sem=hist_send.at[k], recv_sem=hist_recv.at[c],
            device_id=(row, c), device_id_type=MESH,
        ).wait_recv()
        panels = jnp.maximum(col - 1 - c, 0).astype(F32)
        factor = jnp.exp(-rate * (panels * panel)) * jnp.where(c < col, 1.0, 0.0)
        incoming = incoming + hist[c] * factor

    def send(slot_here, slot_there, m, target, sem):
        src = own.at[m] if slot_here is None else win.at[slot_here, m]
        return pltpu.make_async_remote_copy(
            src_ref=src, dst_ref=win.at[slot_there, m], send_sem=sem, recv_sem=recv_sem.at[slot_there, m],
            device_id=(target, col), device_id_type=MESH,
        )

    sends = []
    for m in range(chunks):
        state = incoming * jnp.exp(-rate * float(LEN * m))
        if m > 0:
            state = state + states[(m - 1) * bases : m * bases, :]
        state_high, state_low = split(weights * state)
        carried = jnp.concatenate([state_high, state_low, state_high, state_low], axis=0)
        for t in range(n_types // TILE):
            rows = slice(t * TILE, (t + 1) * TILE)
            piece = amounts[rows, m * LEN : (m + 1) * LEN]
            inside = jnp.dot(
                jnp.concatenate([piece, piece], axis=1), table[...], preferred_element_type=F32
            )
            drive = lax.dot_general(
                carried[:, rows], entry3[...], (((0,), (0,)), ((), ())), preferred_element_type=F32
            )
            for b in range(bases):
                drive = drive + columns[rows, b : b + 1] * inside[:, b * LEN : (b + 1) * LEN]
            own[m, rows, :] = drive.astype(BF16)
        for k, (there, target) in enumerate(((0, up), (4, down), (1 + 2 * odd, mate))):
            copy = send(None, there, m, target, send_sem.at[k, m])
            copy.start()
            sends.append(copy)

    load_blocks.wait()
    blocks[n_blocks] = jnp.zeros(blocks.shape[1:], BF16)

    def place(step, carry):
        d, rest = step // (brows * brows), lax.rem(step, brows * brows)
        i, q = rest // brows, lax.rem(rest, brows)
        wanted = lax.rem(row + n_rows + d - 2, n_rows) * brows + q
        at = n_blocks
        for s in range(slots):
            at = jnp.where(cols_ref[i, s] == wanted, i * slots + s, at)
        dense[d, pl.ds(pl.multiple_of(i * width, width), width), pl.ds(pl.multiple_of(q * width, width), width)] = (
            blocks[at]
        )
        return carry

    lax.fori_loop(0, 5 * brows * brows, place, 0)

    def multiply(d, m, source, first=False, last=False):
        for t in range(n_types // TILE):
            rows = slice(t * TILE, (t + 1) * TILE)
            part = jnp.dot(dense[d, rows, :], source, preferred_element_type=F32)
            if first:
                part = part + columns[rows, bases : bases + 1]
            else:
                part = part + total[m, rows, :]
            if last:
                part = jnp.maximum(part, 0.0) + jnp.log1p(jnp.exp(-jnp.abs(part)))
                result[m, rows, :] = part.astype(BF16)
            else:
                total[m, rows, :] = part

    def arrived(slot, m):
        send(None, slot, m, mate, send_sem.at[0, m]).wait_recv()

    far, near = 4 - 4 * odd, 4 * odd
    mate_slot, passed_slot = 3 - 2 * odd, 1 + 2 * odd
    outs = []

    def finish(m):
        arrived(passed_slot, m)
        multiply(passed_slot, m, win[passed_slot, m], last=True)
        out = pltpu.make_async_copy(result.at[m], out_hbm.at[:, pl.ds(m * LEN, LEN)], out_sem.at[m])
        out.start()
        outs.append(out)

    for m in range(chunks):
        multiply(2, m, own[m], first=True)
    for m in range(chunks):
        arrived(far, m)
        copy = send(far, 3 - 2 * odd, m, mate, pass_sem.at[m])
        copy.start()
        sends.append(copy)
        multiply(far, m, win[far, m])
        arrived(mate_slot, m)
        multiply(mate_slot, m, win[mate_slot, m])
        if m > 0:
            finish(m - 1)
        arrived(near, m)
        multiply(near, m, win[near, m])
    finish(chunks - 1)
    for copy in sends + hist_copies:
        copy.wait_send()
    for out in outs:
        out.wait()


def local(n_rows, n_tm, counts, col_blocks, kernel, mixing, decay_rate, baseline):
    n_types, panel = counts.shape
    chunks = panel // LEN
    brows, slots, width, _ = kernel.shape
    bases = decay_rate.shape[0]
    vmem, smem, hbm = pltpu.VMEM, pltpu.SMEM, pl.ANY
    dma = pltpu.SemaphoreType.DMA
    return pl.pallas_call(
        functools.partial(body, n_rows, n_tm),
        out_shape=jax.ShapeDtypeStruct((n_types, panel), BF16),
        in_specs=[
            pl.BlockSpec(memory_space=smem),
            pl.BlockSpec(memory_space=smem),
            pl.BlockSpec(memory_space=hbm),
            pl.BlockSpec(memory_space=hbm),
            pl.BlockSpec(memory_space=vmem),
            pl.BlockSpec(memory_space=vmem),
        ],
        out_specs=pl.BlockSpec(memory_space=hbm),
        scratch_shapes=[
            vmem((n_types, panel), jnp.int32),
            vmem((n_types, panel), BF16),
            vmem((brows * slots + 1, width, width), BF16),
            vmem((5, n_types, n_types), BF16),
            vmem((chunks, n_types, LEN), BF16),
            vmem((5, chunks, n_types, LEN), BF16),
            vmem((chunks, n_types, LEN), F32),
            vmem((chunks, n_types, LEN), BF16),
            vmem((2 * LEN, bases * LEN), BF16),
            vmem((4 * bases, LEN), BF16),
            vmem((chunks * bases, n_types), F32),
            vmem((n_tm, bases, n_types), F32),
            vmem((bases, n_types), F32),
            vmem((n_types, 2 * bases), F32),
            dma((2,)),
            dma((chunks,)),
            dma((3, chunks)),
            dma((5, chunks)),
            dma((chunks,)),
            dma((n_tm,)),
            dma((n_tm,)),
        ],
        compiler_params=pltpu.CompilerParams(
            collective_id=0, has_side_effects=True, vmem_limit_bytes=56 * 1024 * 1024
        ),
        cost_estimate=pl.CostEstimate(
            flops=2 * n_types * 5 * n_types * panel, bytes_accessed=12 * 1024 * 1024, transcendentals=0
        ),
    )(decay_rate, col_blocks, counts, kernel.reshape(brows * slots, width, width), mixing, baseline.reshape(1, n_types))


def solution(mesh):
    in_specs = (
        P("rows", "tm"),
        P("rows", None),
        P("rows", None, None, None),
        P(None, "rows"),
        P(),
        P("rows"),
    )
    return jax.shard_map(
        functools.partial(local, mesh.shape["rows"], mesh.shape["tm"]),
        mesh=mesh, in_specs=in_specs, out_specs=P("rows", "tm"), check_vma=False,
    )
```

time: 159 us -> 67.3 us (0.42)
  the two profiles are of different devices: /device:TPU:16 before, /device:TPU:0 now
where the time goes in v1:
time: 67.3 us; the launch traced here: 66 us
  Pallas kernels  63.7 us (95%)
  local copies, waits for them, and re-layouts  2.26 us (3%)
    pallas_call x1, Pallas kernels, local(): pl.pallas_call(functools.partial(body, n_rows, n_tm), out_shape=jax.Shape...  63.7 us
    unnamed x1, local copies, waits for them, and re-layouts  2.26 us

profile of v1, /device:TPU:0, one launch (start us, length us, event | category | flops | bytes accessed | tf_op | source)
XLA Modules:
  0.0 66.0 jit_solution(6133337779678836391)
XLA Ops:
  0.0 63.7 %shard_map.64 = bf16[1024,512]{1,0:T(8,128)(2,1)} custom-call(f32[8]{0:T(128)} %decay_ref.1, s32[8,24]{1,0:T(8,128)} %cols_ref.1, s32[1024,512]{1,0:T(8,128)} %counts_hbm.1, bf16[192,128,128]{2,1,0:T(8,128)(2,1)} %bitcast.2, f32[8,1024]{1,0:T(8,128)} %mixing_ref.1, f32[1,1024]{1,0:T(1,128)} %bitcast.3), custom_call_target="tpu_custom_call" | custom-call | flops 5368709120 | bytes 12582912 | tf_op jit(solution)/shard_map/pallas_call | solution.py:213
  63.7 2.3 %copy.8 = bf16[1024,512]{1,0:T(8,128)(2,1)} copy(bf16[1024,512]{1,0:T(8,128)(2,1)} %shard_map.64) | data formatting | bytes 2097152

commit v2 on v1

--- a/solution.py
+++ b/solution.py
@@ -21,8 +21,8 @@
 
 def body(
     n_rows, n_tm,
-    decay_ref, cols_ref, counts_hbm, kernel_hbm, mixing_ref, baseline_ref, out_hbm,
-    counts, amounts, blocks, dense, own, win, total, result, table, entry3, states, hist, leaving, columns,
+    decay_ref, cols_ref, counts_hbm, kernel_hbm, mixing_hbm, baseline_hbm, out_hbm,
+    mixing_ref, baseline_ref, counts, amounts, blocks, dense, own, win, total, result, table, entry3, states, hist, leaving, columns,
     load_sem, out_sem, send_sem, recv_sem, pass_sem, hist_send, hist_recv,
 ):
     n_types, panel = counts.shape
@@ -39,7 +39,11 @@
 
     load_counts = pltpu.make_async_copy(counts_hbm, counts, load_sem.at[0])
     load_blocks = pltpu.make_async_copy(kernel_hbm, blocks.at[pl.ds(0, n_blocks)], load_sem.at[1])
+    load_mixing = pltpu.make_async_copy(mixing_hbm, mixing_ref, load_sem.at[2])
+    load_baseline = pltpu.make_async_copy(baseline_hbm, baseline_ref, load_sem.at[3])
     load_counts.start()
+    load_mixing.start()
+    load_baseline.start()
     load_blocks.start()
 
     barrier = pltpu.get_barrier_semaphore()
@@ -62,24 +66,6 @@
         exits.append(jnp.where(since < LEN * m, jnp.exp(-rate * jnp.maximum(gap, 0.0)), 0.0))
     exits_high, exits_low = split(jnp.concatenate(exits, axis=0))
     exit_table = jnp.concatenate([exits_high, exits_low], axis=0)
-
-    load_counts.wait()
-    amounts[...] = counts[...].astype(F32).astype(BF16)
-    both = lax.dot_general(
-        exit_table, amounts[...], (((1,), (1,)), ((), ())), preferred_element_type=F32
-    )
-    states[...] = both[: chunks * bases] + both[chunks * bases :]
-    leaving[...] = states[(chunks - 1) * bases :, :]
-    pl.semaphore_wait(barrier, 3 + n_tm - 1)
-
-    hist_copies = []
-    for k, c in enumerate(peers):
-        copy = pltpu.make_async_remote_copy(
-            src_ref=leaving, dst_ref=hist.at[col], send_sem=hist_send.at[k], recv_sem=hist_recv.at[col],
-            device_id=(row, c), device_id_type=MESH,
-        )
-        copy.start()
-        hist_copies.append(copy)
 
     distance = (
         lax.broadcasted_iota(jnp.int32, (LEN, LEN), 1) - lax.broadcasted_iota(jnp.int32, (LEN, LEN), 0)
@@ -92,9 +78,44 @@
     offset = lax.broadcasted_iota(jnp.int32, (bases, LEN), 1).astype(F32)
     entry_high, entry_low = split(jnp.exp(-rate_tile * offset))
     entry3[...] = jnp.concatenate([entry_high, entry_high, entry_low, entry_low], axis=0)
+    load_counts.wait()
+    amounts[...] = counts[...].astype(F32).astype(BF16)
+    both = lax.dot_general(
+        exit_table, amounts[...], (((1,), (1,)), ((), ())), preferred_element_type=F32
+    )
+    states[...] = both[: chunks * bases] + both[chunks * bases :]
+    leaving[...] = states[(chunks - 1) * bases :, :]
+    pl.semaphore_wait(barrier, 3 + n_tm - 1)
+
+    hist_copies = []
+    for k, c in enumerate(peers):
+        copy = pltpu.make_async_remote_copy(
+            src_ref=leaving, dst_ref=hist.at[col], send_sem=hist_send.at[k], recv_sem=hist_recv.at[col],
+            device_id=(row, c), device_id_type=MESH,
+        )
+        copy.start()
+        hist_copies.append(copy)
+
+    load_mixing.wait()
+    load_baseline.wait()
     weights = mixing_ref[...] * rate
     stacked = jnp.concatenate([weights, jnp.broadcast_to(baseline_ref[...], (bases, n_types))], axis=0)
     columns[...] = jnp.transpose(stacked)
+
+
+    def inside_part(m, t):
+        piece = amounts[t * TILE : (t + 1) * TILE, m * LEN : (m + 1) * LEN]
+        inside = jnp.dot(
+            jnp.concatenate([piece, piece], axis=1), table[...], preferred_element_type=F32
+        )
+        drive = columns[t * TILE : (t + 1) * TILE, 0:1] * inside[:, 0:LEN]
+        for b in range(1, bases):
+            drive = drive + columns[t * TILE : (t + 1) * TILE, b : b + 1] * inside[:, b * LEN : (b + 1) * LEN]
+        return drive
+
+    tiles = n_types // TILE
+    for t in range(tiles):
+        total[0, t * TILE : (t + 1) * TILE, :] = inside_part(0, t)
 
     incoming = jnp.zeros((bases, n_types), F32)
     for k, c in enumerate(peers):
@@ -106,37 +127,45 @@
         factor = jnp.exp(-rate * (panels * panel)) * jnp.where(c < col, 1.0, 0.0)
         incoming = incoming + hist[c] * factor
 
-    def send(slot_here, slot_there, m, target, sem):
-        src = own.at[m] if slot_here is None else win.at[slot_here, m]
+    def send(slot_here, slot_there, m, t, target, sem):
+        part = pl.ds(t * TILE, TILE)
+        src = own.at[m, part] if slot_here is None else win.at[slot_here, m, part]
         return pltpu.make_async_remote_copy(
-            src_ref=src, dst_ref=win.at[slot_there, m], send_sem=sem, recv_sem=recv_sem.at[slot_there, m],
-            device_id=(target, col), device_id_type=MESH,
+            src_ref=src, dst_ref=win.at[slot_there, m, part], send_sem=sem,
+            recv_sem=recv_sem.at[slot_there, m, t], device_id=(target, col), device_id_type=MESH,
         )
 
     sends = []
+    first_target = jnp.where(odd == 1, up, down)
+    second_target = jnp.where(odd == 1, down, up)
+    routes = ((4 - 4 * odd, first_target), (1 + 2 * odd, mate))
+
+    def send_near(m):
+        for t in range(tiles):
+            copy = send(None, 4 * odd, m, t, second_target, send_sem.at[2, m, t])
+            copy.start()
+            sends.append(copy)
+
     for m in range(chunks):
         state = incoming * jnp.exp(-rate * float(LEN * m))
         if m > 0:
             state = state + states[(m - 1) * bases : m * bases, :]
         state_high, state_low = split(weights * state)
         carried = jnp.concatenate([state_high, state_low, state_high, state_low], axis=0)
-        for t in range(n_types // TILE):
+        for t in range(tiles):
             rows = slice(t * TILE, (t + 1) * TILE)
-            piece = amounts[rows, m * LEN : (m + 1) * LEN]
-            inside = jnp.dot(
-                jnp.concatenate([piece, piece], axis=1), table[...], preferred_element_type=F32
-            )
-            drive = lax.dot_general(
+            inside = total[0, rows, :] if m == 0 else inside_part(m, t)
+            drive = inside + lax.dot_general(
                 carried[:, rows], entry3[...], (((0,), (0,)), ((), ())), preferred_element_type=F32
             )
-            for b in range(bases):
-                drive = drive + columns[rows, b : b + 1] * inside[:, b * LEN : (b + 1) * LEN]
             own[m, rows, :] = drive.astype(BF16)
-        for k, (there, target) in enumerate(((0, up), (4, down), (1 + 2 * odd, mate))):
-            copy = send(None, there, m, target, send_sem.at[k, m])
-            copy.start()
-            sends.append(copy)
-
+            for k, (there, target) in enumerate(routes):
+                copy = send(None, there, m, t, target, send_sem.at[k, m, t])
+                copy.start()
+                sends.append(copy)
+
+    for n in range(chunks // 2):
+        send_near(n)
     load_blocks.wait()
     blocks[n_blocks] = jnp.zeros(blocks.shape[1:], BF16)
 
@@ -168,35 +197,43 @@
             else:
                 total[m, rows, :] = part
 
+    def piece_arrived(slot, m, t):
+        send(None, slot, m, t, mate, send_sem.at[0, m, t]).wait_recv()
+
     def arrived(slot, m):
-        send(None, slot, m, mate, send_sem.at[0, m]).wait_recv()
+        for t in range(tiles):
+            piece_arrived(slot, m, t)
 
     far, near = 4 - 4 * odd, 4 * odd
     mate_slot, passed_slot = 3 - 2 * odd, 1 + 2 * odd
     outs = []
 
+    def use(slot, m, last=False):
+        arrived(slot, m)
+        multiply(slot, m, win[slot, m], last=last)
+
     def finish(m):
-        arrived(passed_slot, m)
-        multiply(passed_slot, m, win[passed_slot, m], last=True)
+        use(near, m, last=True)
         out = pltpu.make_async_copy(result.at[m], out_hbm.at[:, pl.ds(m * LEN, LEN)], out_sem.at[m])
         out.start()
         outs.append(out)
 
+    for n in range(chunks // 2, chunks):
+        send_near(n)
     for m in range(chunks):
-        multiply(2, m, own[m], first=True)
+        for t in range(tiles):
+            piece_arrived(far, m, t)
+            copy = send(far, 3 - 2 * odd, m, t, mate, pass_sem.at[m, t])
+            copy.start()
+            sends.append(copy)
+            if t == 0:
+                multiply(2, m, own[m], first=True)
+        multiply(far, m, win[far, m])
     for m in range(chunks):
-        arrived(far, m)
-        copy = send(far, 3 - 2 * odd, m, mate, pass_sem.at[m])
-        copy.start()
-        sends.append(copy)
-        multiply(far, m, win[far, m])
-        arrived(mate_slot, m)
-        multiply(mate_slot, m, win[mate_slot, m])
-        if m > 0:
-            finish(m - 1)
-        arrived(near, m)
-        multiply(near, m, win[near, m])
-    finish(chunks - 1)
+        use(mate_slot, m)
+    for m in range(chunks):
+        use(passed_slot, m)
+        finish(m)
     for copy in sends + hist_copies:
         copy.wait_send()
     for out in outs:
@@ -216,13 +253,15 @@
         in_specs=[
             pl.BlockSpec(memory_space=smem),
             pl.BlockSpec(memory_space=smem),
-            pl.BlockSpec(memory_space=hbm),
-            pl.BlockSpec(memory_space=hbm),
-            pl.BlockSpec(memory_space=vmem),
-            pl.BlockSpec(memory_space=vmem),
+            pl.BlockSpec(memory_space=pltpu.HBM),
+            pl.BlockSpec(memory_space=pltpu.HBM),
+            pl.BlockSpec(memory_space=pltpu.HBM),
+            pl.BlockSpec(memory_space=pltpu.HBM),
         ],
         out_specs=pl.BlockSpec(memory_space=hbm),
         scratch_shapes=[
+            vmem((bases, n_types), F32),
+            vmem((1, n_types), F32),
             vmem((n_types, panel), jnp.int32),
             vmem((n_types, panel), BF16),
             vmem((brows * slots + 1, width, width), BF16),
@@ -237,11 +276,11 @@
             vmem((n_tm, bases, n_types), F32),
             vmem((bases, n_types), F32),
             vmem((n_types, 2 * bases), F32),
-            dma((2,)),
+            dma((4,)),
             dma((chunks,)),
-            dma((3, chunks)),
-            dma((5, chunks)),
-            dma((chunks,)),
+            dma((3, chunks, n_types // TILE)),
+            dma((5, chunks, n_types // TILE)),
+            dma((chunks, n_types // TILE)),
             dma((n_tm,)),
             dma((n_tm,)),
         ],

time: 67.3 us -> 64.5 us (0.958); the launches traced: 66 us -> 64.3 us
  Pallas kernels: 63.7 us -> 62.1 us
    pallas_call x1, Pallas kernels: 63.7 us -> 62.1 us  [local(): pl.pallas_call(functools.partial(body, n_rows, n_tm), out_shape=jax.Shape...]
where the time goes in v2:
time: 64.5 us; the launch traced here: 64.3 us
  Pallas kernels  62.1 us (96%)
  local copies, waits for them, and re-layouts  2.26 us (4%)
    pallas_call x1, Pallas kernels, local(): pl.pallas_call(functools.partial(body, n_rows, n_tm), out_shape=jax.Shape...  62.1 us
    unnamed x1, local copies, waits for them, and re-layouts  2.26 us

profile of v2, /device:TPU:0, one launch (start us, length us, event | category | flops | bytes accessed | tf_op | source)
XLA Modules:
  0.0 64.3 jit_solution(3499393703801773480)
XLA Ops:
  0.0 62.1 %shard_map.64 = bf16[1024,512]{1,0:T(8,128)(2,1)} custom-call(f32[8]{0:T(128)} %decay_ref.1, s32[8,24]{1,0:T(8,128)} %cols_ref.1, s32[1024,512]{1,0:T(8,128)} %counts_hbm.1, bf16[192,128,128]{2,1,0:T(8,128)(2,1)} %bitcast.2, f32[8,1024]{1,0:T(8,128)} %mixing_hbm.1, f32[1,1024]{1,0:T(1,128)} %bitcast.3), custom_call_target="tpu_custom_call" | custom-call | flops 5368709120 | bytes 12582912 | tf_op jit(solution)/shard_map/pallas_call | solution.py:250
  62.1 2.3 %copy.8 = bf16[1024,512]{1,0:T(8,128)(2,1)} copy(bf16[1024,512]{1,0:T(8,128)(2,1)} %shard_map.64) | data formatting | bytes 2097152
